TPU v7x, 32 devices: a whole 2x2x4 slice. The times are simulated.
32 devices in a mesh: space: 8 (over z, x), chan: 4 (over y, core).
Axes of the slice: x: 2, y: 2, z: 4, core: 2. Of those that a mesh axis runs over, the one named last changes fastest.
Arguments:
- inputs: bfloat16 [16, 256, 1024], P(None, 'chan', 'space'), may hold values from -6 to 6
- kernel_one: bfloat16 [256, 3, 3, 256], P('chan'), may hold values from -0.125 to 0.125
- kernel_two: bfloat16 [256, 3, 3, 256], P('chan'), may hold values from -0.125 to 0.125
- cotangent: bfloat16 [16, 256, 1024], P(None, 'chan', 'space'), may hold values from -6 to 6
Outputs:
- result: bfloat16 [16, 256, 1024], P(None, 'chan', 'space')
- grad_inputs: bfloat16 [16, 256, 1024], P(None, 'chan', 'space')
- grad_kernel_one: float32 [256, 3, 3, 256], P('chan')
- grad_kernel_two: float32 [256, 3, 3, 256], P('chan')
All inputs are finite; a program needn't handle non-finite values.
Results may differ from a plain program's by a relative error of at most 0.019.
Values may be sent and summed in bfloat16 or wider, within the bound.
A program may use at most 64 MiB of HBM per device.

v0:
```python
import jax
import jax.numpy as jnp
from jax import lax
from jax.sharding import PartitionSpec as P


def with_halo(block, sides, width):
    for axis, dim in sides:
        count = lax.axis_size(axis)
        forward = [(i, i + 1) for i in range(count - 1)]
        backward = [(target, source) for source, target in forward]
        low = lax.ppermute(
            lax.slice_in_dim(block, block.shape[dim] - width, None, axis=dim), axis, forward
        )
        high = lax.ppermute(lax.slice_in_dim(block, 0, width, axis=dim), axis, backward)
        block = jnp.concatenate([low, block, high], axis=dim)
    return block


def framed(values):
    wide = with_halo(values, (("space", 2),), 1)
    return jnp.pad(wide, ((1, 1), (0, 0), (0, 0)))


def valid_conv(padded, kernel):
    return lax.conv_general_dilated(
        padded[None],
        kernel,
        (1, 1),
        "VALID",
        dimension_numbers=("NHCW", "OHWI", "NHCW"),
        preferred_element_type=jnp.float32,
    )[0]


def flipped(kernel):
    return jnp.transpose(kernel[:, ::-1, ::-1], (3, 1, 2, 0))


def silu_slope(preact):
    sigmoid_part = jax.nn.sigmoid(preact)
    return sigmoid_part * (1.0 + preact * (1.0 - sigmoid_part))


def tap_products(padded, gradient):
    height, width = (gradient.shape[0], gradient.shape[2])
    pieces = []
    for row_tap in range(3):
        for col_tap in range(3):
            window = padded[row_tap : row_tap + height, :, col_tap : col_tap + width]
            pieces.append(
                jnp.einsum("hiw,how->oi", window, gradient, preferred_element_type=jnp.float32)
            )
    return jnp.stack(pieces, axis=1).reshape(gradient.shape[1], 3, 3, padded.shape[1])


def spread_out(padded):
    return lax.all_gather(padded, "chan", axis=1, tiled=True)


def backward_collect(padded, kernel):
    return lax.psum_scatter(
        valid_conv(padded, flipped(kernel)).astype(jnp.bfloat16),
        "chan",
        scatter_dimension=1,
        tiled=True,
    ).astype(jnp.float32)


def local(inputs, kernel_one, kernel_two, cotangent):
    framed_input = framed(inputs)
    all_input = spread_out(framed_input)
    pre_one = valid_conv(all_input, kernel_one)
    hidden = jax.nn.silu(pre_one).astype(jnp.bfloat16)
    all_hidden = spread_out(framed(hidden))
    pre_two = valid_conv(all_hidden, kernel_two)
    result = jax.nn.silu(pre_two).astype(jnp.bfloat16)
    grad_two = (cotangent.astype(jnp.float32) * silu_slope(pre_two)).astype(jnp.bfloat16)
    sum_two = tap_products(all_hidden, grad_two)
    grad_hidden = backward_collect(framed(grad_two), kernel_two)
    grad_one = (grad_hidden * silu_slope(pre_one)).astype(jnp.bfloat16)
    sum_one = tap_products(all_input, grad_one)
    grad_inputs = backward_collect(framed(grad_one), kernel_one).astype(jnp.bfloat16)
    sum_one, sum_two = lax.psum((sum_one, sum_two), "space")
    return (result, grad_inputs, sum_one, sum_two)


def solution(mesh):
    in_specs = (
        P(None, "chan", "space"),
        P("chan", None, None, None),
        P("chan", None, None, None),
        P(None, "chan", "space"),
    )
    out_specs = (
        P(None, "chan", "space"),
        P(None, "chan", "space"),
        P("chan", None, None, None),
        P("chan", None, None, None),
    )
    return jax.shard_map(local, mesh=mesh, in_specs=in_specs, out_specs=out_specs, check_vma=False)
```

profile of v0, /device:TPU:0, one launch (start us, length us, event | category | flops | bytes accessed | tf_op | source)
XLA Modules:
  0.0 298.1 jit_solution(694349623031645975)
XLA Ops:
  8.4 4.9 %collective-permute-start = (bf16[16,64,1]{2,1,0:T(8,128)(2,1)S(1)}, bf16[16,64,1]{2,1,0:T(8,128)(2,1)S(1)}, u32[]{:S(2)}, u32[]{:S(2)}) collective-permute-start(bf16[16,64,1]{2,1,0:T(8,128)(2,1)S(1)} %get-tuple-element.22), channel_id=1, source_target_pairs={{0,4},{4,8},{8,12},{12,16},{16,20},{20,24},{24,28},{1,5},{5,9},{9,... | collective-permute-start | bytes 6152 | tf_op jit(solution)/shard_map/ppermute | solution.py:12
  14.6 9.8 %collective-permute-done = bf16[16,64,1]{2,1,0:T(8,128)(2,1)S(1)} collective-permute-done((bf16[16,64,1]{2,1,0:T(8,128)(2,1)S(1)}, bf16[16,64,1]{2,1,0:T(8,128)(2,1)S(1)}, u32[]{:S(2)}, u32[]{:S(2)}) %collective-permute-start) | collective-permute-done | bytes 2080 | tf_op jit(solution)/shard_map/ppermute | solution.py:12
  24.5 2.1 select_maximum_fusion.6
  26.6 26.4 %all-gather.3.cloned.1.call-done = bf16[18,256,130]{2,1,0:T(8,128)(2,1)} async-done(((bf16[18,64,130]{2,1,0:T(8,128)(2,1)}), bf16[18,256,130]{2,1,0:T(8,128)(2,1)}) %all-gather.3.cloned.1.call-update) | async-done | bytes 1198096 | tf_op jit(solution)/shard_map/all_gather | solution.py:58
  53.0 2.8 copy.52
  57.4 2.9 fusion.21
  61.3 3.4 %collective-permute-start.2 = (bf16[16,64,1]{2,1,0:T(8,128)(2,1)S(1)}, bf16[16,64,1]{2,1,0:T(8,128)(2,1)S(1)}, u32[]{:S(2)}, u32[]{:S(2)}) collective-permute-start(bf16[16,64,1]{2,1,0:T(8,128)(2,1)S(1)} %get-tuple-element.20), channel_id=1, source_target_pairs={{0,4},{4,8},{8,12},{12,16},{16,20},{20,24},{24,28},{1,5},{5,9},{9,... | collective-permute-start | bytes 6152 | tf_op jit(solution)/shard_map/ppermute | solution.py:12
  66.0 10.3 %collective-permute-done.2 = bf16[16,64,1]{2,1,0:T(8,128)(2,1)S(1)} collective-permute-done((bf16[16,64,1]{2,1,0:T(8,128)(2,1)S(1)}, bf16[16,64,1]{2,1,0:T(8,128)(2,1)S(1)}, u32[]{:S(2)}, u32[]{:S(2)}) %collective-permute-start.2) | collective-permute-done | bytes 2080 | tf_op jit(solution)/shard_map/ppermute | solution.py:12
  77.4 25.2 %all-gather.5.cloned.1.call-done = bf16[18,256,130]{2,1,0:T(8,128)(2,1)} async-done(((bf16[18,64,130]{2,1,0:T(8,128)(2,1)}), bf16[18,256,130]{2,1,0:T(8,128)(2,1)}) %all-gather.5.cloned.1.call-update) | async-done | bytes 1198096 | tf_op jit(solution)/shard_map/all_gather | solution.py:58
  102.6 2.8 copy.53
  106.4 2.9 fusion.18
  111.6 3.4 %collective-permute-start.4 = (bf16[16,64,1]{2,1,0:T(8,128)(2,1)S(1)}, bf16[16,64,1]{2,1,0:T(8,128)(2,1)S(1)}, u32[]{:S(2)}, u32[]{:S(2)}) collective-permute-start(bf16[16,64,1]{2,1,0:T(8,128)(2,1)S(1)} %get-tuple-element.18), channel_id=1, source_target_pairs={{0,4},{4,8},{8,12},{12,16},{16,20},{20,24},{24,28},{1,5},{5,9},{9,... | collective-permute-start | bytes 6152 | tf_op jit(solution)/shard_map/ppermute | solution.py:12
  116.4 10.1 %collective-permute-done.4 = bf16[16,64,1]{2,1,0:T(8,128)(2,1)S(1)} collective-permute-done((bf16[16,64,1]{2,1,0:T(8,128)(2,1)S(1)}, bf16[16,64,1]{2,1,0:T(8,128)(2,1)S(1)}, u32[]{:S(2)}, u32[]{:S(2)}) %collective-permute-start.4) | collective-permute-done | bytes 2080 | tf_op jit(solution)/shard_map/ppermute | solution.py:12
  130.9 1.8 fusion.33
  137.0 19.9 %reduce-scatter.3.cloned.1.call-done = bf16[16,64,128]{2,1,0:T(8,128)(2,1)} async-done(((bf16[16,256,128]{2,1,0:T(8,128)(2,1)}), bf16[16,64,128]{2,1,0:T(8,128)(2,1)}) %reduce-scatter.3.cloned.1.call-update) | async-done | bytes 262160 | tf_op jit(solution)/shard_map/reduce_scatter | solution.py:62
  158.3 3.4 %collective-permute-start.6 = (bf16[16,64,1]{2,1,0:T(8,128)(2,1)S(1)}, bf16[16,64,1]{2,1,0:T(8,128)(2,1)S(1)}, u32[]{:S(2)}, u32[]{:S(2)}) collective-permute-start(bf16[16,64,1]{2,1,0:T(8,128)(2,1)S(1)} %get-tuple-element.16), channel_id=1, source_target_pairs={{0,4},{4,8},{8,12},{12,16},{16,20},{20,24},{24,28},{1,5},{5,9},{9,... | collective-permute-start | bytes 6152 | tf_op jit(solution)/shard_map/ppermute | solution.py:12
  163.0 2.1 fusion.25
  165.1 7.7 %collective-permute-done.6 = bf16[16,64,1]{2,1,0:T(8,128)(2,1)S(1)} collective-permute-done((bf16[16,64,1]{2,1,0:T(8,128)(2,1)S(1)}, bf16[16,64,1]{2,1,0:T(8,128)(2,1)S(1)}, u32[]{:S(2)}, u32[]{:S(2)}) %collective-permute-start.6) | collective-permute-done | bytes 2080 | tf_op jit(solution)/shard_map/ppermute | solution.py:12
  176.1 2.3 copy.47
  178.7 1.8 fusion.42
  185.6 18.9 %reduce-scatter.5.cloned.1.call-done = bf16[16,64,128]{2,0,1:T(8,128)(2,1)} async-done(((bf16[16,256,128]{2,0,1:T(8,128)(2,1)}), bf16[16,64,128]{2,0,1:T(8,128)(2,1)}) %reduce-scatter.5.cloned.1.call-update) | async-done | bytes 262160 | tf_op jit(solution)/shard_map/reduce_scatter | solution.py:62
  204.5 1.7 copy.48
  206.2 82.5 %all-reduce.7.cloned.1.call-done = (f32[64,3,3,256]{3,0,2,1:T(8,128)}, f32[64,3,3,256]{3,0,2,1:T(8,128)}) async-done(((f32[64,3,3,256]{3,0,2,1:T(8,128)}, f32[64,3,3,256]{3,0,2,1:T(8,128)}), (f32[64,3,3,256]{3,0,2,1:T(8,128)}, f32[64,3,3,256]{3,0,2,1:T(8,128)})) %all-reduce.7.cloned.1.call-update) | async-done | bytes 1179664 | tf_op jit(solution)/shard_map/psum | solution.py:84
  288.7 2.0 copy.74
  (101 shorter events, 32.7 us)
Async XLA Ops:
  7.2 99.2 %copy-start = (bf16[64,3,3,256]{3,0,2,1:T(8,128)(2,1)S(1)}, bf16[64,3,3,256]{3,0,2,1:T(8,128)(2,1)}, u32[]{:S(2)}) copy-start(bf16[64,3,3,256]{3,0,2,1:T(8,128)(2,1)} %param.6) | copy-start | bytes 884740
  7.2 45.8 %all-gather.3.cloned.1.call-start = ((), (), s32[]{:S(2)}) async-start(), calls=%async_computation.2 | async-start | bytes 2949120 | tf_op jit(solution)/shard_map/all_gather | solution.py:58
  8.4 16.0 %collective-permute-start = (bf16[16,64,1]{2,1,0:T(8,128)(2,1)S(1)}, bf16[16,64,1]{2,1,0:T(8,128)(2,1)S(1)}, u32[]{:S(2)}, u32[]{:S(2)}) collective-permute-start(bf16[16,64,1]{2,1,0:T(8,128)(2,1)S(1)} %get-tuple-element.22), channel_id=1, source_target_pairs={{0,4},{4,8},{8,12},{12,16},{16,20},{20,24},{24,28},{1,5},{5,9},{9,... | collective-permute-start | bytes 6152 | tf_op jit(solution)/shard_map/ppermute | solution.py:12
  13.3 11.2 %collective-permute-start.1 = (bf16[16,64,1]{2,1,0:T(8,128)(2,1)S(1)}, bf16[16,64,1]{2,1,0:T(8,128)(2,1)S(1)}, u32[]{:S(2)}, u32[]{:S(2)}) collective-permute-start(bf16[16,64,1]{2,1,0:T(8,128)(2,1)S(1)} %get-tuple-element.23), channel_id=1, source_target_pairs={{4,0},{8,4},{12,8},{16,12},{20,16},{24,20},{28,24},{5,1},{9,5},{13... | collective-permute-start | bytes 6152 | tf_op jit(solution)/shard_map/ppermute | solution.py:15
  26.6 76.1 %all-gather.5.cloned.1.call-start = ((), (), s32[]{:S(2)}) async-start(), calls=%async_computation.3 | async-start | bytes 2949120 | tf_op jit(solution)/shard_map/all_gather | solution.py:58
  56.4 1.0 copy-start.10
  56.4 1.0 copy-start.12
  61.0 16.4 %copy-start.1 = (f32[16,1,128,64]{2,3,0,1:T(8,128)}, f32[16,1,128,64]{2,3,0,1:T(8,128)S(1)}, u32[]{:S(2)}) copy-start(f32[16,1,128,64]{2,3,0,1:T(8,128)S(1)} %copy.49) | copy-start | bytes 1572868
  61.3 15.0 %collective-permute-start.2 = (bf16[16,64,1]{2,1,0:T(8,128)(2,1)S(1)}, bf16[16,64,1]{2,1,0:T(8,128)(2,1)S(1)}, u32[]{:S(2)}, u32[]{:S(2)}) collective-permute-start(bf16[16,64,1]{2,1,0:T(8,128)(2,1)S(1)} %get-tuple-element.20), channel_id=1, source_target_pairs={{0,4},{4,8},{8,12},{12,16},{16,20},{20,24},{24,28},{1,5},{5,9},{9,... | collective-permute-start | bytes 6152 | tf_op jit(solution)/shard_map/ppermute | solution.py:12
  64.7 11.6 %collective-permute-start.3 = (bf16[16,64,1]{2,1,0:T(8,128)(2,1)S(1)}, bf16[16,64,1]{2,1,0:T(8,128)(2,1)S(1)}, u32[]{:S(2)}, u32[]{:S(2)}) collective-permute-start(bf16[16,64,1]{2,1,0:T(8,128)(2,1)S(1)} %get-tuple-element.21), channel_id=1, source_target_pairs={{4,0},{8,4},{12,8},{16,12},{20,16},{24,20},{28,24},{5,1},{9,5},{13... | collective-permute-start | bytes 6152 | tf_op jit(solution)/shard_map/ppermute | solution.py:15
  77.4 79.6 %reduce-scatter.3.cloned.1.call-start = ((), (), s32[]{:S(2)}) async-start(), calls=%async_computation.4 | async-start | bytes 1310720 | tf_op jit(solution)/shard_map/reduce_scatter | solution.py:62
  111.6 14.9 %collective-permute-start.4 = (bf16[16,64,1]{2,1,0:T(8,128)(2,1)S(1)}, bf16[16,64,1]{2,1,0:T(8,128)(2,1)S(1)}, u32[]{:S(2)}, u32[]{:S(2)}) collective-permute-start(bf16[16,64,1]{2,1,0:T(8,128)(2,1)S(1)} %get-tuple-element.18), channel_id=1, source_target_pairs={{0,4},{4,8},{8,12},{12,16},{16,20},{20,24},{24,28},{1,5},{5,9},{9,... | collective-permute-start | bytes 6152 | tf_op jit(solution)/shard_map/ppermute | solution.py:12
  115.0 11.6 %collective-permute-start.5 = (bf16[16,64,1]{2,1,0:T(8,128)(2,1)S(1)}, bf16[16,64,1]{2,1,0:T(8,128)(2,1)S(1)}, u32[]{:S(2)}, u32[]{:S(2)}) collective-permute-start(bf16[16,64,1]{2,1,0:T(8,128)(2,1)S(1)} %get-tuple-element.19), channel_id=1, source_target_pairs={{4,0},{8,4},{12,8},{16,12},{20,16},{24,20},{28,24},{5,1},{9,5},{13... | collective-permute-start | bytes 6152 | tf_op jit(solution)/shard_map/ppermute | solution.py:15
  130.8 2.0 copy-start.4
  130.9 73.6 %reduce-scatter.5.cloned.1.call-start = ((), (), s32[]{:S(2)}) async-start(), calls=%async_computation.5 | async-start | bytes 1310720 | tf_op jit(solution)/shard_map/reduce_scatter | solution.py:62
  134.4 1.7 copy-start.5
  136.0 20.9 %copy-start.2 = (f32[16,1,128,64]{2,3,0,1:T(8,128)S(1)}, f32[16,1,128,64]{2,3,0,1:T(8,128)}, u32[]{:S(2)}) copy-start(f32[16,1,128,64]{2,3,0,1:T(8,128)} %copy-done.1) | copy-start | bytes 1572868
  158.3 14.6 %collective-permute-start.6 = (bf16[16,64,1]{2,1,0:T(8,128)(2,1)S(1)}, bf16[16,64,1]{2,1,0:T(8,128)(2,1)S(1)}, u32[]{:S(2)}, u32[]{:S(2)}) collective-permute-start(bf16[16,64,1]{2,1,0:T(8,128)(2,1)S(1)} %get-tuple-element.16), channel_id=1, source_target_pairs={{0,4},{4,8},{8,12},{12,16},{16,20},{20,24},{24,28},{1,5},{5,9},{9,... | collective-permute-start | bytes 6152 | tf_op jit(solution)/shard_map/ppermute | solution.py:12
  161.7 11.2 %collective-permute-start.7 = (bf16[16,64,1]{2,1,0:T(8,128)(2,1)S(1)}, bf16[16,64,1]{2,1,0:T(8,128)(2,1)S(1)}, u32[]{:S(2)}, u32[]{:S(2)}) collective-permute-start(bf16[16,64,1]{2,1,0:T(8,128)(2,1)S(1)} %get-tuple-element.17), channel_id=1, source_target_pairs={{4,0},{8,4},{12,8},{16,12},{20,16},{24,20},{28,24},{5,1},{9,5},{13... | collective-permute-start | bytes 6152 | tf_op jit(solution)/shard_map/ppermute | solution.py:15
  165.1 8.6 %copy-start.7 = (f32[64,9,256]{2,0,1:T(8,128)}, f32[64,9,256]{2,0,1:T(8,128)S(1)}, u32[]{:S(2)}) copy-start(f32[64,9,256]{2,0,1:T(8,128)S(1)} %fusion.25) | copy-start | bytes 1769476
  173.7 1.0 copy-start.11
  178.4 2.1 copy-start.3
  178.4 110.3 %all-reduce.7.cloned.1.call-start = ((), (), s32[]{:S(2)}) async-start(), calls=%async_computation.6 | async-start | bytes 2359296 | tf_op jit(solution)/shard_map/psum | solution.py:84
  288.7 2.0 copy-start.6
  (2 other events, 1.8 us)
Sparse Core Ops, SparseCore 0:
  26.7 26.2 all-gather.2
  77.5 25.0 all-gather.4
  131.0 25.9 reduce-scatter.2
  178.6 25.8 reduce-scatter.4
  208.4 80.2 all-reduce.6
where the time goes:
time: 299 us; the launch traced here: 298 us
  waiting for transfers between devices  211 us (71%)
  local copies, waits for them, and re-layouts  24.5 us (8%)
  matrix products  21.5 us (7%)
  starting transfers between devices  20.8 us (7%)
  between operations  14.3 us (5%)
  other arithmetic  6.14 us (2%)
    psum x1, waiting for transfers between devices, local(): sum_one, sum_two = lax.psum((sum_one, sum_two), 'space')  82.5 us
    all_gather x2, waiting for transfers between devices, spread_out(): return lax.all_gather(padded, 'chan', axis=1, tiled=True)  51.6 us
    reduce_scatter x2, waiting for transfers between devices, backward_collect(): lax.psum_scatter(valid_conv(padded, flipped(kernel)).astype(jnp.bfloat16)...  38.8 us
    ppermute x4, waiting for transfers between devices, with_halo(): lax.ppermute(lax.slice_in_dim(block, block.shape[dim] - width, None, axis...  37.9 us
    unnamed x36, local copies, waits for them, and re-layouts  16.6 us
    ppermute x4, starting transfers between devices, with_halo(): lax.ppermute(lax.slice_in_dim(block, block.shape[dim] - width, None, axis...  15 us
    dot_general x18, matrix products, tap_products(): jnp.einsum('hiw,how->oi', window, gradient, preferred_element_type=jnp.fl...  13.6 us
    conv_general_dilated x4, matrix products, valid_conv(): lax.conv_general_dilated(padded[None], kernel, (1, 1), 'VALID', dimension...  7.9 us
  transfers between devices with their start and end apart: 13, of which 9 were waited for; matrix products, arithmetic and copies ran while one was open for 5% of the time, Pallas kernels for 0%

commit v1 on v0

v1 whole, which is shorter than its diff:
```python
import functools

import jax
import jax.numpy as jnp
from jax import lax
from jax.experimental import pallas as pl
from jax.experimental.pallas import tpu as pltpu
from jax.sharding import PartitionSpec as P

F32 = jnp.float32
BF16 = jnp.bfloat16
MESH = pl.DeviceIdType.MESH
LANES = 128
CHUNKS = 4


def kernel(
    n, reduce_here, x_ref, k1_ref, k2_ref, cot_ref, result_ref, gin_ref, g1_ref, g2_ref,
    blocks, halo_in, halo_out, cat_one, cat_two, cat_back, weight, partial, slope_one,
    grad_rows, kt_out, kt_in, sum_out, sum_in, sum_all,
    st_send, st_recv, halo_send, halo_recv, kt_send, kt_recv, rs_send, rs_recv, ag_send, ag_recv,
):
    s, c = lax.axis_index("space"), lax.axis_index("chan")
    rows, chans = x_ref.shape[0], x_ref.shape[1]
    full = 4 * chans
    wide = 3 * full
    left, right = lax.rem(s + n - 1, n), lax.rem(s + 1, n)
    sibling = c + 1 - 2 * lax.rem(c, 2)
    across = lax.rem(c + 2, 4)
    lane = lax.broadcasted_iota(jnp.int32, (chans, LANES), 1)
    lane_full = lax.broadcasted_iota(jnp.int32, (full, LANES), 1)

    def remote(src, dst, send, recv, to_s, to_c):
        return pltpu.make_async_remote_copy(
            src_ref=src, dst_ref=dst, send_sem=send, recv_sem=recv,
            device_id={"space": to_s, "chan": to_c}, device_id_type=MESH,
        )

    barrier = pltpu.get_barrier_semaphore()
    count = 0
    for d in range(1, 4):
        pl.semaphore_signal(barrier, inc=1, device_id={"space": s, "chan": lax.rem(c + d, 4)}, device_id_type=MESH)
        count += 1
    for side in (left, right):
        for j in range(4):
            pl.semaphore_signal(barrier, inc=1, device_id={"space": side, "chan": j}, device_id_type=MESH)
            count += 1
    if reduce_here:
        for d in range(2, n - 1):
            pl.semaphore_signal(barrier, inc=1, device_id={"space": lax.rem(s + d, n), "chan": c}, device_id_type=MESH)
            count += 1

    def edge_step(p, value, low, high):
        low = jnp.where(lane == p, pltpu.roll(value, p, 1), low)
        high = jnp.where(lane == p, pltpu.roll(value, lax.rem(p + 1, LANES), 1), high)
        return low, high

    zero_edge = jnp.zeros((chans, LANES), F32)
    pending = []

    def send_stage(t, low, high):
        halo_out[t, 0] = low.astype(BF16)
        halo_out[t, 1] = high.astype(BF16)
        started = []
        for j in range(4):
            for side, to in ((0, left), (1, right)):
                copy = remote(
                    halo_out.at[t, side], halo_in.at[t, 1 - side, c],
                    halo_send.at[t, side, j], halo_recv.at[t, 1 - side, c], to, j,
                )
                copy.start()
                pending.append(copy)
        step = rows // CHUNKS
        across_copies, near_copies = [], []
        for k in range(CHUNKS):
            part = pl.ds(k * step, step)
            copy = remote(
                blocks.at[t, c, part], blocks.at[t, c, part],
                st_send.at[t, 0, k], st_recv.at[t, 0, k], s, across,
            )
            copy.start()
            pending.append(copy)
            across_copies.append(copy)
        for k in range(CHUNKS):
            part = pl.ds(k * step, step)
            copy = remote(
                blocks.at[t, c, part], blocks.at[t, c, part],
                st_send.at[t, 1, k], st_recv.at[t, 1, k], s, sibling,
            )
            copy.start()
            pending.append(copy)
            near_copies.append(copy)
        return across_copies, near_copies

    def forward_stage(t, copies):
        across_copies, near_copies = copies
        step = rows // CHUNKS
        forwards = []
        for k in range(CHUNKS):
            across_copies[k].wait_recv()
            part = pl.ds(k * step, step)
            copy = remote(
                blocks.at[t, across, part], blocks.at[t, across, part],
                st_send.at[t, 2, k], st_recv.at[t, 2, k], s, sibling,
            )
            copy.start()
            pending.append(copy)
            forwards.append(copy)
        return forwards + near_copies

    def collect_stage(t, waits, cat):
        for j in range(4):
            for side in range(2):
                remote(
                    halo_out.at[t, side], halo_in.at[t, side, j],
                    halo_send.at[t, side, j], halo_recv.at[t, side, j], left, j,
                ).wait_recv()
        for copy in waits:
            copy.wait_recv()
        from_left = halo_in[t, 0].reshape(full, LANES).astype(F32)
        from_right = halo_in[t, 1].reshape(full, LANES).astype(F32)
        from_left = jnp.where(s > 0, from_left, 0.0)
        from_right = jnp.where(s < n - 1, from_right, 0.0)
        cat[:, 0:LANES] = jnp.zeros((wide, LANES), BF16)
        cat[:, (rows + 1) * LANES:] = jnp.zeros((wide, LANES), BF16)

        def body(p, _):
            value = blocks[t, :, p].reshape(full, LANES)
            value32 = value.astype(F32)
            at = pl.ds(pl.multiple_of((p + 1) * LANES, LANES), LANES)
            low = jnp.where(
                lane_full == 0, pltpu.roll(from_left, lax.rem(LANES - p, LANES), 1), pltpu.roll(value32, 1, 1)
            )
            high = jnp.where(
                lane_full == LANES - 1, pltpu.roll(from_right, LANES - 1 - p, 1), pltpu.roll(value32, LANES - 1, 1)
            )
            cat[0:full, at] = low.astype(BF16)
            cat[full:2 * full, at] = value
            cat[2 * full:, at] = high.astype(BF16)
            return 0

        lax.fori_loop(0, rows, body, 0)

    def conv(cat):
        def body(t, _):
            at = pl.ds(pl.multiple_of(t * 2 * LANES, 2 * LANES), 2 * LANES)
            partial[:, at] = jnp.dot(weight[...], cat[:, at], preferred_element_type=F32)
            return 0

        lax.fori_loop(0, (rows + 2) // 2, body, 0)

    def preact(p):
        total = None
        for a in range(3):
            at = pl.ds(pl.multiple_of((p + a) * LANES, LANES), LANES)
            term = partial[a * chans:(a + 1) * chans, at]
            total = term if total is None else total + term
        return total

    def set_weight(k_ref):
        for a in range(3):
            weight[a * chans:(a + 1) * chans, :] = k_ref[:, a * wide:(a + 1) * wide]

    def put_grad(p, value):
        for a in range(3):
            at = pl.ds(pl.multiple_of((p + a) * LANES, LANES), LANES)
            grad_rows[a * chans:(a + 1) * chans, at] = value

    def sum_piece(k):
        return (
            pl.ds(pl.multiple_of((k // 2) * 16, 16), 16),
            pl.ds(pl.multiple_of(lax.rem(k, 2) * (3 * wide // 2), LANES), 3 * wide // 2),
        )

    def kernel_gradient(layer, cat, out_ref):
        total = lax.dot_general(
            grad_rows[...], cat[...], (((1,), (1,)), ((), ())), preferred_element_type=F32
        )
        if not reduce_here:
            for a in range(3):
                out_ref[:, a * wide:(a + 1) * wide] = total[a * chans:(a + 1) * chans]
            return []
        for a in range(3):
            sum_out[layer, :, a * wide:(a + 1) * wide] = total[a * chans:(a + 1) * chans].astype(BF16)
        copies = []
        for d in range(1, n):
            to = lax.rem(s + d, n)
            rr, ll = sum_piece(to)
            copy = remote(
                sum_out.at[layer, rr, ll], sum_in.at[layer, d],
                rs_send.at[layer, d], rs_recv.at[layer, d], to, c,
            )
            copy.start()
            pending.append(copy)
            copies.append(copy)
        return copies

    def kernel_sum(layer, copies):
        rr, ll = sum_piece(s)
        total = sum_out[layer, rr, ll].astype(F32)
        for d in range(1, n):
            copies[d - 1].wait_recv()
            total = total + sum_in[layer, d].astype(F32)
        sum_all[layer, rr, ll] = total.astype(BF16)
        out = []
        for d in range(1, n):
            to = lax.rem(s + d, n)
            copy = remote(
                sum_all.at[layer, rr, ll], sum_all.at[layer, rr, ll],
                ag_send.at[layer, d], ag_recv.at[layer, d], to, c,
            )
            copy.start()
            pending.append(copy)
            out.append(copy)
        return out

    def send_taps(layer):
        copies = []
        for d in range(1, 4):
            copy = remote(
                kt_out.at[layer, lax.rem(c + d, 4)], kt_in.at[layer, c],
                kt_send.at[layer, d], kt_recv.at[layer, d], s, lax.rem(c + d, 4),
            )
            copy.start()
            pending.append(copy)
            copies.append(copy)
        return copies

    def set_back_weight(layer, copies):
        for copy in copies:
            copy.wait_recv()
        taps = kt_in[layer].reshape(full, kt_in.shape[3]).astype(F32).T.astype(BF16)
        for a in range(3):
            for b in range(3):
                tap = (2 - a) * 3 + 2 - b
                weight[a * chans:(a + 1) * chans, b * full:(b + 1) * full] = taps[tap * chans:(tap + 1) * chans]

    def first(p, edges):
        value = x_ref[p]
        blocks[0, c, p] = value
        return edge_step(p, value.astype(F32), *edges)

    low, high = lax.fori_loop(0, rows, first, (zero_edge, zero_edge))
    pl.semaphore_wait(barrier, count)
    copies = send_stage(0, low, high)
    for layer, k_ref in ((0, k1_ref), (1, k2_ref)):
        for j in range(4):
            for tap in range(9):
                kt_out[layer, j, :, tap * chans:(tap + 1) * chans] = (
                    k_ref[:, tap * full + j * chans:tap * full + (j + 1) * chans]
                )
            kt_out[layer, j, :, 9 * chans:] = jnp.zeros((chans, kt_out.shape[3] - 9 * chans), BF16)
        kt_in[layer, c] = kt_out[layer, c]
    back_two = send_taps(1)
    set_weight(k1_ref)
    grad_rows[...] = jnp.zeros(grad_rows.shape, BF16)
    collect_stage(0, forward_stage(0, copies), cat_one)
    conv(cat_one)

    def second(p, edges):
        pre = preact(p)
        sig = jax.nn.sigmoid(pre)
        slope_one[p] = sig * (1.0 + pre * (1.0 - sig))
        value = (pre * sig).astype(BF16)
        blocks[1, c, p] = value
        return edge_step(p, value.astype(F32), *edges)

    low, high = lax.fori_loop(0, rows, second, (zero_edge, zero_edge))

    copies = send_stage(1, low, high)
    back_one = send_taps(0)
    set_weight(k2_ref)
    collect_stage(1, forward_stage(1, copies), cat_two)
    conv(cat_two)

    def third(p, edges):
        pre = preact(p)
        sig = jax.nn.sigmoid(pre)
        result_ref[p] = (pre * sig).astype(BF16)
        value = (cot_ref[p].astype(F32) * (sig * (1.0 + pre * (1.0 - sig)))).astype(BF16)
        blocks[2, c, p] = value
        put_grad(p, value)
        return edge_step(p, value.astype(F32), *edges)

    low, high = lax.fori_loop(0, rows, third, (zero_edge, zero_edge))

    copies = send_stage(2, low, high)
    set_back_weight(1, back_two)
    reduce_two = kernel_gradient(1, cat_two, g2_ref)
    collect_stage(2, forward_stage(2, copies), cat_back)
    conv(cat_back)

    def fourth(p, edges):
        value = (preact(p) * slope_one[p]).astype(BF16)
        blocks[3, c, p] = value
        put_grad(p, value)
        return edge_step(p, value.astype(F32), *edges)

    low, high = lax.fori_loop(0, rows, fourth, (zero_edge, zero_edge))

    copies = send_stage(3, low, high)
    reduce_one = kernel_gradient(0, cat_one, g1_ref)
    set_back_weight(0, back_one)
    waits = forward_stage(3, copies)
    gather_two = kernel_sum(1, reduce_two) if reduce_here else []
    gather_one = kernel_sum(0, reduce_one) if reduce_here else []
    collect_stage(3, waits, cat_back)
    conv(cat_back)

    def last(p, _):
        gin_ref[p] = preact(p).astype(BF16)
        return 0

    lax.fori_loop(0, rows, last, 0)

    if reduce_here:
        for layer, out, ref in ((1, gather_two, g2_ref), (0, gather_one, g1_ref)):
            for copy in out:
                copy.wait_recv()
            ref[...] = sum_all[layer].astype(F32)
    for copy in pending:
        copy.wait_send()


def local(n, inputs, kernel_one, kernel_two, cotangent):
    rows, chans, cols = inputs.shape
    full = 4 * chans
    wide = 3 * full
    reduce_here = n == 8
    lanes = (rows + 2) * LANES
    taps = -(-9 * chans // LANES) * LANES
    dma = pltpu.SemaphoreType.DMA
    vmem = pl.BlockSpec(memory_space=pltpu.VMEM)
    result, grad_inputs, sum_one, sum_two = pl.pallas_call(
        functools.partial(kernel, n, reduce_here),
        out_shape=(
            jax.ShapeDtypeStruct((rows, chans, cols), BF16),
            jax.ShapeDtypeStruct((rows, chans, cols), BF16),
            jax.ShapeDtypeStruct((chans, 3 * wide), F32),
            jax.ShapeDtypeStruct((chans, 3 * wide), F32),
        ),
        in_specs=[vmem] * 4,
        out_specs=[vmem] * 4,
        scratch_shapes=[
            pltpu.VMEM((4, 4, rows, chans, LANES), BF16),
            pltpu.VMEM((4, 2, 4, chans, LANES), BF16),
            pltpu.VMEM((4, 2, chans, LANES), BF16),
            pltpu.VMEM((wide, lanes), BF16),
            pltpu.VMEM((wide, lanes), BF16),
            pltpu.VMEM((wide, lanes), BF16),
            pltpu.VMEM((3 * chans, wide), BF16),
            pltpu.VMEM((3 * chans, lanes), F32),
            pltpu.VMEM((rows, chans, LANES), F32),
            pltpu.VMEM((3 * chans, lanes), BF16),
            pltpu.VMEM((2, 4, chans, taps), BF16),
            pltpu.VMEM((2, 4, chans, taps), BF16),
            pltpu.VMEM((2, chans, 3 * wide), BF16),
            pltpu.VMEM((2, 8, 16, 3 * wide // 2), BF16),
            pltpu.VMEM((2, chans, 3 * wide), BF16),
            dma((4, 3, CHUNKS)),
            dma((4, 3, CHUNKS)),
            dma((4, 2, 4)),
            dma((4, 2, 4)),
            dma((2, 4)),
            dma((2, 4)),
            dma((2, 8)),
            dma((2, 8)),
            dma((2, 8)),
            dma((2, 8)),
        ],
        compiler_params=pltpu.CompilerParams(
            collective_id=0, has_side_effects=True, vmem_limit_bytes=48 * 1024 * 1024
        ),
    )(
        inputs,
        kernel_one.reshape(chans, 3 * wide),
        kernel_two.reshape(chans, 3 * wide),
        cotangent,
    )
    sum_one = sum_one.reshape(chans, 3, 3, full)
    sum_two = sum_two.reshape(chans, 3, 3, full)
    if not reduce_here:
        sum_one, sum_two = lax.psum((sum_one, sum_two), "space")
    return result, grad_inputs, sum_one, sum_two


def solution(mesh):
    act = P(None, "chan", "space")
    ker = P("chan", None, None, None)
    return jax.shard_map(
        functools.partial(local, mesh.shape["space"]), mesh=mesh,
        in_specs=(act, ker, ker, act), out_specs=(act, act, ker, ker), check_vma=False,
    )
```

time: 299 us -> 86.3 us (0.29)
  waiting for transfers between devices: 211 us -> 0 us
  Pallas kernels: 0 us -> 78.1 us
  matrix products: 21.5 us -> 0 us
  starting transfers between devices: 20.8 us -> 0 us
  local copies, waits for them, and re-layouts: 24.5 us -> 7.31 us
  between operations: 14.3 us -> 0.69 us
  other arithmetic: 6.14 us -> 0 us
    psum x1 -> x0, waiting for transfers between devices: 82.5 us -> none  [local(): sum_one, sum_two = lax.psum((sum_one, sum_two), 'space')]
    pallas_call x0 -> x1, Pallas kernels: none -> 78.1 us  [local(): pl.pallas_call(functools.partial(kernel, n, reduce_here), out_shape=(jax....]
    all_gather x2 -> x0, waiting for transfers between devices: 51.6 us -> none  [spread_out(): return lax.all_gather(padded, 'chan', axis=1, tiled=True)]
    reduce_scatter x2 -> x0, waiting for transfers between devices: 38.8 us -> none  [backward_collect(): lax.psum_scatter(valid_conv(padded, flipped(kernel)).astype(jnp.bfloat16)...]
    ppermute x8 -> x0, waiting for transfers between devices: 37.9 us -> none  [the longest x4 37.9 us: with_halo(): lax.ppermute(lax.slice_in_dim(block, block.shape[dim] - width, None, axis...]
    ppermute x8 -> x0, starting transfers between devices: 20.4 us -> none  [the longest x4 15 us: with_halo(): lax.ppermute(lax.slice_in_dim(block, block.shape[dim] - width, None, axis...]
    dot_general x18 -> x0, matrix products: 13.6 us -> none  [tap_products(): jnp.einsum('hiw,how->oi', window, gradient, preferred_element_type=jnp.fl...]
    unnamed x36 -> x12, local copies, waits for them, and re-layouts: 16.6 us -> 6.01 us
  transfers between devices with their start and end apart: 13 -> 0, of which waited for: 9 -> 0; matrix products, arithmetic and copies ran while one was open for 5% -> 0% of each run, Pallas kernels for 0% -> 0%
where the time goes in v1:
time: 86.3 us; the launch traced here: 86.1 us
  Pallas kernels  78.1 us (90%)
  local copies, waits for them, and re-layouts  7.31 us (8%)
    pallas_call x1, Pallas kernels, local(): pl.pallas_call(functools.partial(kernel, n, reduce_here), out_shape=(jax....  78.1 us
    unnamed x12, local copies, waits for them, and re-layouts  6.01 us

profile of v1, /device:TPU:0, one launch (start us, length us, event | category | flops | bytes accessed | tf_op | source)
XLA Modules:
  0.0 86.1 jit_solution(9994416382400407220)
XLA Ops:
  0.6 1.2 %copy.12 = bf16[64,3,3,256]{3,2,1,0:T(4,128)(2,1)S(1)} copy(bf16[64,3,3,256]{3,0,2,1:T(8,128)(2,1)} %param.5) | data formatting | bytes 589824 | tf_op args[1]
  1.9 0.0 copy-start.2
  1.9 0.3 reshape.20.k1_ref
  2.2 0.6 copy-done.2
  2.8 0.3 copy.13
  3.1 0.0 copy-start
  3.1 0.0 copy-start.1
  3.1 0.3 reshape.21.k2_ref
  3.4 0.6 copy-done
  4.0 0.1 copy-done.1
  4.1 78.1 %shard_map.75 = (bf16[16,64,128]{2,1,0:T(8,128)(2,1)S(1)}, bf16[16,64,128]{2,1,0:T(8,128)(2,1)S(1)}, f32[64,2304]{1,0:T(8,128)S(1)}, f32[64,2304]{1,0:T(8,128)S(1)}) custom-call(bf16[16,64,128]{2,1,0:T(8,128)(2,1)S(1)} %copy-done, bf16[64,2304]{1,0:T(8,128)(2,1)S(1)} %reshape.20.k1_ref, bf16[64,2304]{1,0:T(8,128)(2,1)S(1)} %reshape.21.k2_ref, ...), custom_call_target="tpu_custom_call" | custom-call | tf_op jit(solution)/shard_map/pallas_call | solution.py:334
  82.2 0.3 reshape.22
  82.5 0.9 %copy.14 = f32[64,3,3,256]{3,0,2,1:T(8,128)} copy(f32[64,3,3,256]{3,2,1,0:T(4,128)S(1)} %reshape.22) | data formatting | bytes 1179648
  83.4 0.3 reshape.23
  83.7 0.9 %copy.15 = f32[64,3,3,256]{3,0,2,1:T(8,128)} copy(f32[64,3,3,256]{3,2,1,0:T(4,128)S(1)} %reshape.23) | data formatting | bytes 1179648
  84.7 0.7 copy.18
  85.4 0.7 copy.19
Async XLA Ops:
  1.9 1.0 %copy-start.2 = (bf16[64,3,3,256]{3,0,2,1:T(8,128)(2,1)S(1)}, bf16[64,3,3,256]{3,0,2,1:T(8,128)(2,1)}, u32[]{:S(2)}) copy-start(bf16[64,3,3,256]{3,0,2,1:T(8,128)(2,1)} %param.6) | copy-start | bytes 884740
  3.1 1.0 %copy-start = (bf16[16,64,128]{2,1,0:T(8,128)(2,1)S(1)}, bf16[16,64,128]{2,1,0:T(8,128)(2,1)}, u32[]{:S(2)}) copy-start(bf16[16,64,128]{2,1,0:T(8,128)(2,1)} %x_ref.1) | copy-start | bytes 786436
  3.1 1.0 %copy-start.1 = (bf16[16,64,128]{2,1,0:T(8,128)(2,1)S(1)}, bf16[16,64,128]{2,1,0:T(8,128)(2,1)}, u32[]{:S(2)}) copy-start(bf16[16,64,128]{2,1,0:T(8,128)(2,1)} %cot_ref.1) | copy-start | bytes 786436

commit v2 on v1

--- a/solution.py
+++ b/solution.py
@@ -17,13 +17,14 @@
 def kernel(
     n, reduce_here, x_ref, k1_ref, k2_ref, cot_ref, result_ref, gin_ref, g1_ref, g2_ref,
     blocks, halo_in, halo_out, cat_one, cat_two, cat_back, weight, partial, slope_one,
-    grad_rows, kt_out, kt_in, sum_out, sum_in, sum_all,
+    edges, grad_rows, kt_out, kt_in, sum_out, sum_in, sum_all,
     st_send, st_recv, halo_send, halo_recv, kt_send, kt_recv, rs_send, rs_recv, ag_send, ag_recv,
 ):
     s, c = lax.axis_index("space"), lax.axis_index("chan")
     rows, chans = x_ref.shape[0], x_ref.shape[1]
     full = 4 * chans
     wide = 3 * full
+    high_piece = 9 * chans // 4
     left, right = lax.rem(s + n - 1, n), lax.rem(s + 1, n)
     sibling = c + 1 - 2 * lax.rem(c, 2)
     across = lax.rem(c + 2, 4)
@@ -92,9 +93,31 @@
             near_copies.append(copy)
         return across_copies, near_copies
 
-    def forward_stage(t, copies):
+    def collect_stage(t, copies, cat, hook=None):
         across_copies, near_copies = copies
         step = rows // CHUNKS
+        cat[:, 0:LANES] = jnp.zeros((wide, LANES), BF16)
+        cat[:, (rows + 1) * LANES:] = jnp.zeros((wide, LANES), BF16)
+        partial[:, 0:LANES] = jnp.zeros((3 * chans, LANES), F32)
+        partial[:, (rows + 1) * LANES:] = jnp.zeros((3 * chans, LANES), F32)
+
+        def row_step(p, _):
+            value = blocks[t, :, p].reshape(full, LANES)
+            at = pl.ds(pl.multiple_of((p + 1) * LANES, LANES), LANES)
+            edge_low = pltpu.roll(edges[0], lax.rem(LANES - p, LANES), 1)
+            edge_high = pltpu.roll(edges[1], LANES - 1 - p, 1)
+            cat[0:full, at] = jnp.where(lane_full == 0, edge_low, pltpu.roll(value, 1, 1))
+            cat[full:2 * full, at] = value
+            cat[2 * full:, at] = jnp.where(lane_full == LANES - 1, edge_high, pltpu.roll(value, LANES - 1, 1))
+            return 0
+
+        def work(k):
+            near_copies[k].wait_recv()
+            forwards[k].wait_recv()
+            lax.fori_loop(k * step, (k + 1) * step, row_step, 0, unroll=True)
+            at = slice((k * step + 1) * LANES, ((k + 1) * step + 1) * LANES)
+            partial[:, at] = jnp.dot(weight[...], cat[:, at], preferred_element_type=F32)
+
         forwards = []
         for k in range(CHUNKS):
             across_copies[k].wait_recv()
@@ -106,48 +129,22 @@
             copy.start()
             pending.append(copy)
             forwards.append(copy)
-        return forwards + near_copies
-
-    def collect_stage(t, waits, cat):
-        for j in range(4):
-            for side in range(2):
-                remote(
-                    halo_out.at[t, side], halo_in.at[t, side, j],
-                    halo_send.at[t, side, j], halo_recv.at[t, side, j], left, j,
-                ).wait_recv()
-        for copy in waits:
-            copy.wait_recv()
-        from_left = halo_in[t, 0].reshape(full, LANES).astype(F32)
-        from_right = halo_in[t, 1].reshape(full, LANES).astype(F32)
-        from_left = jnp.where(s > 0, from_left, 0.0)
-        from_right = jnp.where(s < n - 1, from_right, 0.0)
-        cat[:, 0:LANES] = jnp.zeros((wide, LANES), BF16)
-        cat[:, (rows + 1) * LANES:] = jnp.zeros((wide, LANES), BF16)
-
-        def body(p, _):
-            value = blocks[t, :, p].reshape(full, LANES)
-            value32 = value.astype(F32)
-            at = pl.ds(pl.multiple_of((p + 1) * LANES, LANES), LANES)
-            low = jnp.where(
-                lane_full == 0, pltpu.roll(from_left, lax.rem(LANES - p, LANES), 1), pltpu.roll(value32, 1, 1)
-            )
-            high = jnp.where(
-                lane_full == LANES - 1, pltpu.roll(from_right, LANES - 1 - p, 1), pltpu.roll(value32, LANES - 1, 1)
-            )
-            cat[0:full, at] = low.astype(BF16)
-            cat[full:2 * full, at] = value
-            cat[2 * full:, at] = high.astype(BF16)
-            return 0
-
-        lax.fori_loop(0, rows, body, 0)
-
-    def conv(cat):
-        def body(t, _):
-            at = pl.ds(pl.multiple_of(t * 2 * LANES, 2 * LANES), 2 * LANES)
-            partial[:, at] = jnp.dot(weight[...], cat[:, at], preferred_element_type=F32)
-            return 0
-
-        lax.fori_loop(0, (rows + 2) // 2, body, 0)
+            if k == 0:
+                for j in range(4):
+                    for side in range(2):
+                        remote(
+                            halo_out.at[t, side], halo_in.at[t, side, j],
+                            halo_send.at[t, side, j], halo_recv.at[t, side, j], left, j,
+                        ).wait_recv()
+                from_left = halo_in[t, 0].reshape(full, LANES).astype(F32)
+                from_right = halo_in[t, 1].reshape(full, LANES).astype(F32)
+                edges[0] = jnp.where(s > 0, from_left, 0.0).astype(BF16)
+                edges[1] = jnp.where(s < n - 1, from_right, 0.0).astype(BF16)
+            else:
+                work(k - 1)
+        gathered = hook() if hook is not None else []
+        work(CHUNKS - 1)
+        return gathered
 
     def preact(p):
         total = None
@@ -159,7 +156,8 @@
 
     def set_weight(k_ref):
         for a in range(3):
-            weight[a * chans:(a + 1) * chans, :] = k_ref[:, a * wide:(a + 1) * wide]
+            for b in range(3):
+                weight[a * chans:(a + 1) * chans, b * full:(b + 1) * full] = k_ref[3 * a + b]
 
     def put_grad(p, value):
         for a in range(3):
@@ -168,20 +166,24 @@
 
     def sum_piece(k):
         return (
-            pl.ds(pl.multiple_of((k // 2) * 16, 16), 16),
-            pl.ds(pl.multiple_of(lax.rem(k, 2) * (3 * wide // 2), LANES), 3 * wide // 2),
+            pl.ds(pl.multiple_of((k // 2) * high_piece, 16), high_piece),
+            pl.ds(pl.multiple_of(lax.rem(k, 2) * LANES, LANES), LANES),
         )
 
     def kernel_gradient(layer, cat, out_ref):
         total = lax.dot_general(
             grad_rows[...], cat[...], (((1,), (1,)), ((), ())), preferred_element_type=F32
         )
+        for a in range(3):
+            for b in range(3):
+                tap = 3 * a + b
+                term = total[a * chans:(a + 1) * chans, b * full:(b + 1) * full]
+                if reduce_here:
+                    sum_out[layer, tap * chans:(tap + 1) * chans, :] = term.astype(BF16)
+                else:
+                    out_ref[tap * chans:(tap + 1) * chans, :] = term
         if not reduce_here:
-            for a in range(3):
-                out_ref[:, a * wide:(a + 1) * wide] = total[a * chans:(a + 1) * chans]
             return []
-        for a in range(3):
-            sum_out[layer, :, a * wide:(a + 1) * wide] = total[a * chans:(a + 1) * chans].astype(BF16)
         copies = []
         for d in range(1, n):
             to = lax.rem(s + d, n)
@@ -240,22 +242,21 @@
         blocks[0, c, p] = value
         return edge_step(p, value.astype(F32), *edges)
 
-    low, high = lax.fori_loop(0, rows, first, (zero_edge, zero_edge))
+    low, high = lax.fori_loop(0, rows, first, (zero_edge, zero_edge), unroll=4)
     pl.semaphore_wait(barrier, count)
     copies = send_stage(0, low, high)
     for layer, k_ref in ((0, k1_ref), (1, k2_ref)):
         for j in range(4):
             for tap in range(9):
                 kt_out[layer, j, :, tap * chans:(tap + 1) * chans] = (
-                    k_ref[:, tap * full + j * chans:tap * full + (j + 1) * chans]
+                    k_ref[tap, :, j * chans:(j + 1) * chans]
                 )
             kt_out[layer, j, :, 9 * chans:] = jnp.zeros((chans, kt_out.shape[3] - 9 * chans), BF16)
         kt_in[layer, c] = kt_out[layer, c]
     back_two = send_taps(1)
     set_weight(k1_ref)
     grad_rows[...] = jnp.zeros(grad_rows.shape, BF16)
-    collect_stage(0, forward_stage(0, copies), cat_one)
-    conv(cat_one)
+    collect_stage(0, copies, cat_one)
 
     def second(p, edges):
         pre = preact(p)
@@ -265,13 +266,12 @@
         blocks[1, c, p] = value
         return edge_step(p, value.astype(F32), *edges)
 
-    low, high = lax.fori_loop(0, rows, second, (zero_edge, zero_edge))
+    low, high = lax.fori_loop(0, rows, second, (zero_edge, zero_edge), unroll=4)
 
     copies = send_stage(1, low, high)
     back_one = send_taps(0)
     set_weight(k2_ref)
-    collect_stage(1, forward_stage(1, copies), cat_two)
-    conv(cat_two)
+    collect_stage(1, copies, cat_two)
 
     def third(p, edges):
         pre = preact(p)
@@ -282,13 +282,14 @@
         put_grad(p, value)
         return edge_step(p, value.astype(F32), *edges)
 
-    low, high = lax.fori_loop(0, rows, third, (zero_edge, zero_edge))
+    low, high = lax.fori_loop(0, rows, third, (zero_edge, zero_edge), unroll=4)
 
     copies = send_stage(2, low, high)
     set_back_weight(1, back_two)
     reduce_two = kernel_gradient(1, cat_two, g2_ref)
-    collect_stage(2, forward_stage(2, copies), cat_back)
-    conv(cat_back)
+    gather_two = collect_stage(
+        2, copies, cat_back, functools.partial(kernel_sum, 1, reduce_two) if reduce_here else None
+    )
 
     def fourth(p, edges):
         value = (preact(p) * slope_one[p]).astype(BF16)
@@ -296,16 +297,14 @@
         put_grad(p, value)
         return edge_step(p, value.astype(F32), *edges)
 
-    low, high = lax.fori_loop(0, rows, fourth, (zero_edge, zero_edge))
+    low, high = lax.fori_loop(0, rows, fourth, (zero_edge, zero_edge), unroll=4)
 
     copies = send_stage(3, low, high)
     reduce_one = kernel_gradient(0, cat_one, g1_ref)
     set_back_weight(0, back_one)
-    waits = forward_stage(3, copies)
-    gather_two = kernel_sum(1, reduce_two) if reduce_here else []
-    gather_one = kernel_sum(0, reduce_one) if reduce_here else []
-    collect_stage(3, waits, cat_back)
-    conv(cat_back)
+    gather_one = collect_stage(
+        3, copies, cat_back, functools.partial(kernel_sum, 0, reduce_one) if reduce_here else None
+    )
 
     def last(p, _):
         gin_ref[p] = preact(p).astype(BF16)
@@ -336,8 +335,8 @@
         out_shape=(
             jax.ShapeDtypeStruct((rows, chans, cols), BF16),
             jax.ShapeDtypeStruct((rows, chans, cols), BF16),
-            jax.ShapeDtypeStruct((chans, 3 * wide), F32),
-            jax.ShapeDtypeStruct((chans, 3 * wide), F32),
+            jax.ShapeDtypeStruct((9 * chans, full), F32),
+            jax.ShapeDtypeStruct((9 * chans, full), F32),
         ),
         in_specs=[vmem] * 4,
         out_specs=[vmem] * 4,
@@ -351,12 +350,13 @@
             pltpu.VMEM((3 * chans, wide), BF16),
             pltpu.VMEM((3 * chans, lanes), F32),
             pltpu.VMEM((rows, chans, LANES), F32),
+            pltpu.VMEM((2, full, LANES), BF16),
             pltpu.VMEM((3 * chans, lanes), BF16),
             pltpu.VMEM((2, 4, chans, taps), BF16),
             pltpu.VMEM((2, 4, chans, taps), BF16),
-            pltpu.VMEM((2, chans, 3 * wide), BF16),
-            pltpu.VMEM((2, 8, 16, 3 * wide // 2), BF16),
-            pltpu.VMEM((2, chans, 3 * wide), BF16),
+            pltpu.VMEM((2, 9 * chans, full), BF16),
+            pltpu.VMEM((2, 8, 9 * chans // 4, LANES), BF16),
+            pltpu.VMEM((2, 9 * chans, full), BF16),
             dma((4, 3, CHUNKS)),
             dma((4, 3, CHUNKS)),
             dma((4, 2, 4)),
@@ -373,12 +373,12 @@
         ),
     )(
         inputs,
-        kernel_one.reshape(chans, 3 * wide),
-        kernel_two.reshape(chans, 3 * wide),
+        kernel_one.transpose(1, 2, 0, 3).reshape(9, chans, full),
+        kernel_two.transpose(1, 2, 0, 3).reshape(9, chans, full),
         cotangent,
     )
-    sum_one = sum_one.reshape(chans, 3, 3, full)
-    sum_two = sum_two.reshape(chans, 3, 3, full)
+    sum_one = sum_one.reshape(3, 3, chans, full).transpose(2, 0, 1, 3)
+    sum_two = sum_two.reshape(3, 3, chans, full).transpose(2, 0, 1, 3)
     if not reduce_here:
         sum_one, sum_two = lax.psum((sum_one, sum_two), "space")
     return result, grad_inputs, sum_one, sum_two

time: 86.3 us -> 70.6 us (0.82)
  Pallas kernels: 78.1 us -> 62.6 us
    pallas_call x1, Pallas kernels: 78.1 us -> 62.6 us  [local(): pl.pallas_call(functools.partial(kernel, n, reduce_here), out_shape=(jax....]
    reshape x4 -> x0, local copies, waits for them, and re-layouts: 1.3 us -> none  [the longest x1 0.34 us: local(): kernel_one.reshape(chans, 3 * wide)]
where the time goes in v2:
time: 70.6 us; the launch traced here: 70.1 us
  Pallas kernels  62.6 us (89%)
  local copies, waits for them, and re-layouts  6.85 us (10%)
    pallas_call x1, Pallas kernels, local(): pl.pallas_call(functools.partial(kernel, n, reduce_here), out_shape=(jax....  62.6 us
    unnamed x12, local copies, waits for them, and re-layouts  6.85 us

profile of v2, /device:TPU:0, one launch (start us, length us, event | category | flops | bytes accessed | tf_op | source)
XLA Modules:
  0.0 70.1 jit_solution(14476484833313937779)
XLA Ops:
  0.6 0.0 copy-start
  0.6 1.0 %copy-done = bf16[64,3,3,256]{3,0,2,1:T(8,128)(2,1)S(1)} copy-done((bf16[64,3,3,256]{3,0,2,1:T(8,128)(2,1)S(1)}, bf16[64,3,3,256]{3,0,2,1:T(8,128)(2,1)}, u32[]{:S(2)}) %copy-start) | copy-done | bytes 294936
  1.6 0.0 copy-start.1
  1.6 1.0 %copy-done.1 = bf16[64,3,3,256]{3,0,2,1:T(8,128)(2,1)S(1)} copy-done((bf16[64,3,3,256]{3,0,2,1:T(8,128)(2,1)S(1)}, bf16[64,3,3,256]{3,0,2,1:T(8,128)(2,1)}, u32[]{:S(2)}) %copy-start.1) | copy-done | bytes 294936
  2.6 0.0 copy-start.2
  2.6 0.9 %copy-done.2 = bf16[16,64,128]{2,1,0:T(8,128)(2,1)S(1)} copy-done((bf16[16,64,128]{2,1,0:T(8,128)(2,1)S(1)}, bf16[16,64,128]{2,1,0:T(8,128)(2,1)}, u32[]{:S(2)}) %copy-start.2) | copy-done | bytes 262168
  3.5 0.0 copy-start.3
  3.5 0.9 %copy-done.3 = bf16[16,64,128]{2,1,0:T(8,128)(2,1)S(1)} copy-done((bf16[16,64,128]{2,1,0:T(8,128)(2,1)S(1)}, bf16[16,64,128]{2,1,0:T(8,128)(2,1)}, u32[]{:S(2)}) %copy-start.3) | copy-done | bytes 262168
  4.5 62.6 %shard_map.75 = (bf16[16,64,128]{2,1,0:T(8,128)(2,1)S(1)}, bf16[16,64,128]{2,1,0:T(8,128)(2,1)S(1)}, f32[576,256]{1,0:T(8,128)S(1)}, f32[576,256]{1,0:T(8,128)S(1)}) custom-call(bf16[16,64,128]{2,1,0:T(8,128)(2,1)S(1)} %copy-done.2, bf16[9,64,256]{2,1,0:T(8,128)(2,1)S(1)} %bitcast.14, bf16[9,64,256]{2,1,0:T(8,128)(2,1)S(1)} %bitcast.15, ...), custom_call_target="tpu_custom_call" | custom-call | tf_op jit(solution)/shard_map/pallas_call | solution.py:333
  67.1 0.7 %copy.12 = bf16[16,64,128]{2,1,0:T(8,128)(2,1)} copy(bf16[16,64,128]{2,1,0:T(8,128)(2,1)S(1)} %get-tuple-element.16) | data formatting | bytes 524288
  67.8 0.7 %copy.13 = bf16[16,64,128]{2,1,0:T(8,128)(2,1)} copy(bf16[16,64,128]{2,1,0:T(8,128)(2,1)S(1)} %get-tuple-element.17) | data formatting | bytes 524288
  68.5 0.8 %copy.14 = f32[64,3,3,256]{3,0,2,1:T(8,128)} copy(f32[64,3,3,256]{3,0,2,1:T(8,128)S(1)} %bitcast.13) | data formatting | bytes 1179648
  69.3 0.8 %copy.15 = f32[64,3,3,256]{3,0,2,1:T(8,128)} copy(f32[64,3,3,256]{3,0,2,1:T(8,128)S(1)} %bitcast.12) | data formatting | bytes 1179648
Async XLA Ops:
  0.6 1.0 %copy-start = (bf16[64,3,3,256]{3,0,2,1:T(8,128)(2,1)S(1)}, bf16[64,3,3,256]{3,0,2,1:T(8,128)(2,1)}, u32[]{:S(2)}) copy-start(bf16[64,3,3,256]{3,0,2,1:T(8,128)(2,1)} %param.5) | copy-start | bytes 884740
  1.6 1.0 %copy-start.1 = (bf16[64,3,3,256]{3,0,2,1:T(8,128)(2,1)S(1)}, bf16[64,3,3,256]{3,0,2,1:T(8,128)(2,1)}, u32[]{:S(2)}) copy-start(bf16[64,3,3,256]{3,0,2,1:T(8,128)(2,1)} %param.6) | copy-start | bytes 884740
  2.6 0.9 %copy-start.2 = (bf16[16,64,128]{2,1,0:T(8,128)(2,1)S(1)}, bf16[16,64,128]{2,1,0:T(8,128)(2,1)}, u32[]{:S(2)}) copy-start(bf16[16,64,128]{2,1,0:T(8,128)(2,1)} %x_ref.1) | copy-start | bytes 786436
  3.5 0.9 %copy-start.3 = (bf16[16,64,128]{2,1,0:T(8,128)(2,1)S(1)}, bf16[16,64,128]{2,1,0:T(8,128)(2,1)}, u32[]{:S(2)}) copy-start(bf16[16,64,128]{2,1,0:T(8,128)(2,1)} %cot_ref.1) | copy-start | bytes 786436

commit v3 on v2

--- a/solution.py
+++ b/solution.py
@@ -59,10 +59,9 @@
     zero_edge = jnp.zeros((chans, LANES), F32)
     pending = []
 
-    def send_stage(t, low, high):
+    def send_halo(t, low, high):
         halo_out[t, 0] = low.astype(BF16)
         halo_out[t, 1] = high.astype(BF16)
-        started = []
         for j in range(4):
             for side, to in ((0, left), (1, right)):
                 copy = remote(
@@ -71,29 +70,20 @@
                 )
                 copy.start()
                 pending.append(copy)
+
+    def send_chunk(t, k, copies):
         step = rows // CHUNKS
-        across_copies, near_copies = [], []
-        for k in range(CHUNKS):
-            part = pl.ds(k * step, step)
+        part = pl.ds(k * step, step)
+        for held, way, to in zip(copies, (0, 1), (across, sibling)):
             copy = remote(
                 blocks.at[t, c, part], blocks.at[t, c, part],
-                st_send.at[t, 0, k], st_recv.at[t, 0, k], s, across,
-            )
-            copy.start()
-            pending.append(copy)
-            across_copies.append(copy)
-        for k in range(CHUNKS):
-            part = pl.ds(k * step, step)
-            copy = remote(
-                blocks.at[t, c, part], blocks.at[t, c, part],
-                st_send.at[t, 1, k], st_recv.at[t, 1, k], s, sibling,
-            )
-            copy.start()
-            pending.append(copy)
-            near_copies.append(copy)
-        return across_copies, near_copies
-
-    def collect_stage(t, copies, cat, hook=None):
+                st_send.at[t, way, k], st_recv.at[t, way, k], s, to,
+            )
+            copy.start()
+            pending.append(copy)
+            held.append(copy)
+
+    def collect_stage(t, copies, cat, act, hook=None):
         across_copies, near_copies = copies
         step = rows // CHUNKS
         cat[:, 0:LANES] = jnp.zeros((wide, LANES), BF16)
@@ -116,9 +106,12 @@
             forwards[k].wait_recv()
             lax.fori_loop(k * step, (k + 1) * step, row_step, 0, unroll=True)
             at = slice((k * step + 1) * LANES, ((k + 1) * step + 1) * LANES)
-            partial[:, at] = jnp.dot(weight[...], cat[:, at], preferred_element_type=F32)
-
-        forwards = []
+            partial[:, at] = jnp.dot(weight[t], cat[:, at], preferred_element_type=F32)
+
+        def rows_done(k, edge):
+            return lax.fori_loop(k * step, (k + 1) * step, act, edge, unroll=True)
+
+        edge, later, forwards = (zero_edge, zero_edge), ([], []), []
         for k in range(CHUNKS):
             across_copies[k].wait_recv()
             part = pl.ds(k * step, step)
@@ -142,9 +135,19 @@
                 edges[1] = jnp.where(s < n - 1, from_right, 0.0).astype(BF16)
             else:
                 work(k - 1)
+            if k >= 2:
+                edge = rows_done(k - 2, edge)
+                if t < 3:
+                    send_chunk(t + 1, k - 2, later)
         gathered = hook() if hook is not None else []
         work(CHUNKS - 1)
-        return gathered
+        edge = rows_done(CHUNKS - 2, edge)
+        edge = rows_done(CHUNKS - 1, edge)
+        if t < 3:
+            send_halo(t + 1, *edge)
+            send_chunk(t + 1, CHUNKS - 2, later)
+            send_chunk(t + 1, CHUNKS - 1, later)
+        return later, gathered
 
     def preact(p):
         total = None
@@ -154,10 +157,10 @@
             total = term if total is None else total + term
         return total
 
-    def set_weight(k_ref):
+    def set_weight(t, k_ref):
         for a in range(3):
             for b in range(3):
-                weight[a * chans:(a + 1) * chans, b * full:(b + 1) * full] = k_ref[3 * a + b]
+                weight[t, a * chans:(a + 1) * chans, b * full:(b + 1) * full] = k_ref[3 * a + b]
 
     def put_grad(p, value):
         for a in range(3):
@@ -235,7 +238,34 @@
         for a in range(3):
             for b in range(3):
                 tap = (2 - a) * 3 + 2 - b
-                weight[a * chans:(a + 1) * chans, b * full:(b + 1) * full] = taps[tap * chans:(tap + 1) * chans]
+                weight[3 - layer, a * chans:(a + 1) * chans, b * full:(b + 1) * full] = taps[tap * chans:(tap + 1) * chans]
+
+    def second(p, edges):
+        pre = preact(p)
+        sig = jax.nn.sigmoid(pre)
+        slope_one[p] = sig * (1.0 + pre * (1.0 - sig))
+        value = (pre * sig).astype(BF16)
+        blocks[1, c, p] = value
+        return edge_step(p, value.astype(F32), *edges)
+
+    def third(p, edges):
+        pre = preact(p)
+        sig = jax.nn.sigmoid(pre)
+        result_ref[p] = (pre * sig).astype(BF16)
+        value = (cot_ref[p].astype(F32) * (sig * (1.0 + pre * (1.0 - sig)))).astype(BF16)
+        blocks[2, c, p] = value
+        put_grad(p, value)
+        return edge_step(p, value.astype(F32), *edges)
+
+    def fourth(p, edges):
+        value = (preact(p) * slope_one[p]).astype(BF16)
+        blocks[3, c, p] = value
+        put_grad(p, value)
+        return edge_step(p, value.astype(F32), *edges)
+
+    def last(p, edges):
+        gin_ref[p] = preact(p).astype(BF16)
+        return edges
 
     def first(p, edges):
         value = x_ref[p]
@@ -244,7 +274,10 @@
 
     low, high = lax.fori_loop(0, rows, first, (zero_edge, zero_edge), unroll=4)
     pl.semaphore_wait(barrier, count)
-    copies = send_stage(0, low, high)
+    send_halo(0, low, high)
+    copies = ([], [])
+    for k in range(CHUNKS):
+        send_chunk(0, k, copies)
     for layer, k_ref in ((0, k1_ref), (1, k2_ref)):
         for j in range(4):
             for tap in range(9):
@@ -254,69 +287,35 @@
             kt_out[layer, j, :, 9 * chans:] = jnp.zeros((chans, kt_out.shape[3] - 9 * chans), BF16)
         kt_in[layer, c] = kt_out[layer, c]
     back_two = send_taps(1)
-    set_weight(k1_ref)
+    set_weight(0, k1_ref)
+    set_weight(1, k2_ref)
     grad_rows[...] = jnp.zeros(grad_rows.shape, BF16)
-    collect_stage(0, copies, cat_one)
-
-    def second(p, edges):
-        pre = preact(p)
-        sig = jax.nn.sigmoid(pre)
-        slope_one[p] = sig * (1.0 + pre * (1.0 - sig))
-        value = (pre * sig).astype(BF16)
-        blocks[1, c, p] = value
-        return edge_step(p, value.astype(F32), *edges)
-
-    low, high = lax.fori_loop(0, rows, second, (zero_edge, zero_edge), unroll=4)
-
-    copies = send_stage(1, low, high)
+    copies, _ = collect_stage(0, copies, cat_one, second)
+
+
     back_one = send_taps(0)
-    set_weight(k2_ref)
-    collect_stage(1, copies, cat_two)
-
-    def third(p, edges):
-        pre = preact(p)
-        sig = jax.nn.sigmoid(pre)
-        result_ref[p] = (pre * sig).astype(BF16)
-        value = (cot_ref[p].astype(F32) * (sig * (1.0 + pre * (1.0 - sig)))).astype(BF16)
-        blocks[2, c, p] = value
-        put_grad(p, value)
-        return edge_step(p, value.astype(F32), *edges)
-
-    low, high = lax.fori_loop(0, rows, third, (zero_edge, zero_edge), unroll=4)
-
-    copies = send_stage(2, low, high)
     set_back_weight(1, back_two)
+    copies, _ = collect_stage(1, copies, cat_two, third)
+
+
     reduce_two = kernel_gradient(1, cat_two, g2_ref)
-    gather_two = collect_stage(
-        2, copies, cat_back, functools.partial(kernel_sum, 1, reduce_two) if reduce_here else None
+    set_back_weight(0, back_one)
+    copies, gather_two = collect_stage(
+        2, copies, cat_back, fourth, functools.partial(kernel_sum, 1, reduce_two) if reduce_here else None
     )
 
-    def fourth(p, edges):
-        value = (preact(p) * slope_one[p]).astype(BF16)
-        blocks[3, c, p] = value
-        put_grad(p, value)
-        return edge_step(p, value.astype(F32), *edges)
-
-    low, high = lax.fori_loop(0, rows, fourth, (zero_edge, zero_edge), unroll=4)
-
-    copies = send_stage(3, low, high)
+
     reduce_one = kernel_gradient(0, cat_one, g1_ref)
-    set_back_weight(0, back_one)
-    gather_one = collect_stage(
-        3, copies, cat_back, functools.partial(kernel_sum, 0, reduce_one) if reduce_here else None
+    _, gather_one = collect_stage(
+        3, copies, cat_back, last, functools.partial(kernel_sum, 0, reduce_one) if reduce_here else None
     )
 
-    def last(p, _):
-        gin_ref[p] = preact(p).astype(BF16)
-        return 0
-
-    lax.fori_loop(0, rows, last, 0)
 
     if reduce_here:
         for layer, out, ref in ((1, gather_two, g2_ref), (0, gather_one, g1_ref)):
             for copy in out:
                 copy.wait_recv()
-            ref[...] = sum_all[layer].astype(F32)
+            ref[...] = sum_all[layer]
     for copy in pending:
         copy.wait_send()
 
@@ -335,8 +334,8 @@
         out_shape=(
             jax.ShapeDtypeStruct((rows, chans, cols), BF16),
             jax.ShapeDtypeStruct((rows, chans, cols), BF16),
-            jax.ShapeDtypeStruct((9 * chans, full), F32),
-            jax.ShapeDtypeStruct((9 * chans, full), F32),
+            jax.ShapeDtypeStruct((9 * chans, full), BF16 if reduce_here else F32),
+            jax.ShapeDtypeStruct((9 * chans, full), BF16 if reduce_here else F32),
         ),
         in_specs=[vmem] * 4,
         out_specs=[vmem] * 4,
@@ -347,7 +346,7 @@
             pltpu.VMEM((wide, lanes), BF16),
             pltpu.VMEM((wide, lanes), BF16),
             pltpu.VMEM((wide, lanes), BF16),
-            pltpu.VMEM((3 * chans, wide), BF16),
+            pltpu.VMEM((4, 3 * chans, wide), BF16),
             pltpu.VMEM((3 * chans, lanes), F32),
             pltpu.VMEM((rows, chans, LANES), F32),
             pltpu.VMEM((2, full, LANES), BF16),
@@ -377,8 +376,8 @@
         kernel_two.transpose(1, 2, 0, 3).reshape(9, chans, full),
         cotangent,
     )
-    sum_one = sum_one.reshape(3, 3, chans, full).transpose(2, 0, 1, 3)
-    sum_two = sum_two.reshape(3, 3, chans, full).transpose(2, 0, 1, 3)
+    sum_one = sum_one.astype(F32).reshape(3, 3, chans, full).transpose(2, 0, 1, 3)
+    sum_two = sum_two.astype(F32).reshape(3, 3, chans, full).transpose(2, 0, 1, 3)
     if not reduce_here:
         sum_one, sum_two = lax.psum((sum_one, sum_two), "space")
     return result, grad_inputs, sum_one, sum_two

time: 70.6 us -> 69.3 us (0.982)
  local copies, waits for them, and re-layouts: 6.85 us -> 5.22 us
  other arithmetic: 0 us -> 1.14 us
    unnamed x12 -> x10, local copies, waits for them, and re-layouts: 6.85 us -> 5.22 us
    transpose x0 -> x1, other arithmetic: none -> 1.14 us  [local(): sum_two.astype(F32).reshape(3, 3, chans, full).transpose(2, 0, 1, 3)]
where the time goes in v3:
time: 69.3 us; the launch traced here: 69.1 us
  Pallas kernels  62 us (89%)
  local copies, waits for them, and re-layouts  5.22 us (8%)
  other arithmetic  1.14 us (2%)
    pallas_call x1, Pallas kernels, local(): pl.pallas_call(functools.partial(kernel, n, reduce_here), out_shape=(jax....  62 us
    unnamed x10, local copies, waits for them, and re-layouts  5.22 us

profile of v3, /device:TPU:0, one launch (start us, length us, event | category | flops | bytes accessed | tf_op | source)
XLA Modules:
  0.0 69.1 jit_solution(6215416937387927295)
XLA Ops:
  0.6 0.0 copy-start
  0.6 1.0 %copy-done = bf16[64,3,3,256]{3,0,2,1:T(8,128)(2,1)S(1)} copy-done((bf16[64,3,3,256]{3,0,2,1:T(8,128)(2,1)S(1)}, bf16[64,3,3,256]{3,0,2,1:T(8,128)(2,1)}, u32[]{:S(2)}) %copy-start) | copy-done | bytes 294936
  1.6 0.0 copy-start.1
  1.6 1.0 %copy-done.1 = bf16[64,3,3,256]{3,0,2,1:T(8,128)(2,1)S(1)} copy-done((bf16[64,3,3,256]{3,0,2,1:T(8,128)(2,1)S(1)}, bf16[64,3,3,256]{3,0,2,1:T(8,128)(2,1)}, u32[]{:S(2)}) %copy-start.1) | copy-done | bytes 294936
  2.6 0.0 copy-start.2
  2.6 0.9 %copy-done.2 = bf16[16,64,128]{2,1,0:T(8,128)(2,1)S(1)} copy-done((bf16[16,64,128]{2,1,0:T(8,128)(2,1)S(1)}, bf16[16,64,128]{2,1,0:T(8,128)(2,1)}, u32[]{:S(2)}) %copy-start.2) | copy-done | bytes 262168
  3.5 0.0 copy-start.3
  3.5 0.9 %copy-done.3 = bf16[16,64,128]{2,1,0:T(8,128)(2,1)S(1)} copy-done((bf16[16,64,128]{2,1,0:T(8,128)(2,1)S(1)}, bf16[16,64,128]{2,1,0:T(8,128)(2,1)}, u32[]{:S(2)}) %copy-start.3) | copy-done | bytes 262168
  4.5 62.0 %shard_map.75 = (bf16[16,64,128]{2,1,0:T(8,128)(2,1)S(1)}, bf16[16,64,128]{2,1,0:T(8,128)(2,1)S(1)}, bf16[576,256]{1,0:T(8,128)(2,1)S(1)}, bf16[576,256]{1,0:T(8,128)(2,1)S(1)}) custom-call(bf16[16,64,128]{2,1,0:T(8,128)(2,1)S(1)} %copy-done.2, bf16[9,64,256]{2,1,0:T(8,128)(2,1)S(1)} %bitcast.16, bf16[9,64,256]{2,1,0:T(8,128)(2,1)S(1)} %bitcast.17, ...), custom_call_target="tpu_custom_call" | custom-call | tf_op jit(solution)/shard_map/pallas_call | solution.py:332
  66.5 1.1 %convert_bitcast_fusion = (f32[64,3,3,256]{3,0,2,1:T(8,128)}, f32[64,3,3,256]{3,0,2,1:T(8,128)}) fusion(bf16[3,3,64,256]{3,2,1,0:T(8,128)(2,1)S(1)} %bitcast.15, bf16[3,3,64,256]{3,2,1,0:T(8,128)(2,1)S(1)} %bitcast.14), kind=kLoop, calls=%fused_computation | loop fusion | flops 294912 | bytes 1769472 | tf_op jit(solution)/shard_map/transpose | solution.py:380
  67.7 0.7 %copy.10 = bf16[16,64,128]{2,1,0:T(8,128)(2,1)} copy(bf16[16,64,128]{2,1,0:T(8,128)(2,1)S(1)} %get-tuple-element.18) | data formatting | bytes 524288
  68.4 0.7 %copy.11 = bf16[16,64,128]{2,1,0:T(8,128)(2,1)} copy(bf16[16,64,128]{2,1,0:T(8,128)(2,1)S(1)} %get-tuple-element.19) | data formatting | bytes 524288
Async XLA Ops:
  0.6 1.0 %copy-start = (bf16[64,3,3,256]{3,0,2,1:T(8,128)(2,1)S(1)}, bf16[64,3,3,256]{3,0,2,1:T(8,128)(2,1)}, u32[]{:S(2)}) copy-start(bf16[64,3,3,256]{3,0,2,1:T(8,128)(2,1)} %param.5) | copy-start | bytes 884740
  1.6 1.0 %copy-start.1 = (bf16[64,3,3,256]{3,0,2,1:T(8,128)(2,1)S(1)}, bf16[64,3,3,256]{3,0,2,1:T(8,128)(2,1)}, u32[]{:S(2)}) copy-start(bf16[64,3,3,256]{3,0,2,1:T(8,128)(2,1)} %param.6) | copy-start | bytes 884740
  2.6 0.9 %copy-start.2 = (bf16[16,64,128]{2,1,0:T(8,128)(2,1)S(1)}, bf16[16,64,128]{2,1,0:T(8,128)(2,1)}, u32[]{:S(2)}) copy-start(bf16[16,64,128]{2,1,0:T(8,128)(2,1)} %x_ref.1) | copy-start | bytes 786436
  3.5 0.9 %copy-start.3 = (bf16[16,64,128]{2,1,0:T(8,128)(2,1)S(1)}, bf16[16,64,128]{2,1,0:T(8,128)(2,1)}, u32[]{:S(2)}) copy-start(bf16[16,64,128]{2,1,0:T(8,128)(2,1)} %cot_ref.1) | copy-start | bytes 786436

commit v4 on v3

--- a/solution.py
+++ b/solution.py
@@ -142,10 +142,11 @@
         gathered = hook() if hook is not None else []
         work(CHUNKS - 1)
         edge = rows_done(CHUNKS - 2, edge)
+        if t < 3:
+            send_chunk(t + 1, CHUNKS - 2, later)
         edge = rows_done(CHUNKS - 1, edge)
         if t < 3:
             send_halo(t + 1, *edge)
-            send_chunk(t + 1, CHUNKS - 2, later)
             send_chunk(t + 1, CHUNKS - 1, later)
         return later, gathered
 

time: 69.3 us -> 69.3 us (level)
  no operation moved by 1% of the time
where the time goes in v4:
time: 69.3 us; the launch traced here: 69 us
  Pallas kernels  62 us (89%)
  local copies, waits for them, and re-layouts  5.22 us (8%)
  other arithmetic  1.14 us (2%)
    pallas_call x1, Pallas kernels, local(): pl.pallas_call(functools.partial(kernel, n, reduce_here), out_shape=(jax....  62 us
    unnamed x10, local copies, waits for them, and re-layouts  5.22 us

profile of v4, /device:TPU:0, one launch (start us, length us, event | category | flops | bytes accessed | tf_op | source)
XLA Modules:
  0.0 69.0 jit_solution(5911664507054620534)
XLA Ops:
  0.6 0.0 copy-start
  0.6 1.0 %copy-done = bf16[64,3,3,256]{3,0,2,1:T(8,128)(2,1)S(1)} copy-done((bf16[64,3,3,256]{3,0,2,1:T(8,128)(2,1)S(1)}, bf16[64,3,3,256]{3,0,2,1:T(8,128)(2,1)}, u32[]{:S(2)}) %copy-start) | copy-done | bytes 294936
  1.6 0.0 copy-start.1
  1.6 1.0 %copy-done.1 = bf16[64,3,3,256]{3,0,2,1:T(8,128)(2,1)S(1)} copy-done((bf16[64,3,3,256]{3,0,2,1:T(8,128)(2,1)S(1)}, bf16[64,3,3,256]{3,0,2,1:T(8,128)(2,1)}, u32[]{:S(2)}) %copy-start.1) | copy-done | bytes 294936
  2.6 0.0 copy-start.2
  2.6 0.9 %copy-done.2 = bf16[16,64,128]{2,1,0:T(8,128)(2,1)S(1)} copy-done((bf16[16,64,128]{2,1,0:T(8,128)(2,1)S(1)}, bf16[16,64,128]{2,1,0:T(8,128)(2,1)}, u32[]{:S(2)}) %copy-start.2) | copy-done | bytes 262168
  3.5 0.0 copy-start.3
  3.5 0.9 %copy-done.3 = bf16[16,64,128]{2,1,0:T(8,128)(2,1)S(1)} copy-done((bf16[16,64,128]{2,1,0:T(8,128)(2,1)S(1)}, bf16[16,64,128]{2,1,0:T(8,128)(2,1)}, u32[]{:S(2)}) %copy-start.3) | copy-done | bytes 262168
  4.5 62.0 %shard_map.75 = (bf16[16,64,128]{2,1,0:T(8,128)(2,1)S(1)}, bf16[16,64,128]{2,1,0:T(8,128)(2,1)S(1)}, bf16[576,256]{1,0:T(8,128)(2,1)S(1)}, bf16[576,256]{1,0:T(8,128)(2,1)S(1)}) custom-call(bf16[16,64,128]{2,1,0:T(8,128)(2,1)S(1)} %copy-done.2, bf16[9,64,256]{2,1,0:T(8,128)(2,1)S(1)} %bitcast.16, bf16[9,64,256]{2,1,0:T(8,128)(2,1)S(1)} %bitcast.17, ...), custom_call_target="tpu_custom_call" | custom-call | tf_op jit(solution)/shard_map/pallas_call | solution.py:333
  66.5 1.1 %convert_bitcast_fusion = (f32[64,3,3,256]{3,0,2,1:T(8,128)}, f32[64,3,3,256]{3,0,2,1:T(8,128)}) fusion(bf16[3,3,64,256]{3,2,1,0:T(8,128)(2,1)S(1)} %bitcast.15, bf16[3,3,64,256]{3,2,1,0:T(8,128)(2,1)S(1)} %bitcast.14), kind=kLoop, calls=%fused_computation | loop fusion | flops 294912 | bytes 1769472 | tf_op jit(solution)/shard_map/transpose | solution.py:381
  67.6 0.7 %copy.10 = bf16[16,64,128]{2,1,0:T(8,128)(2,1)} copy(bf16[16,64,128]{2,1,0:T(8,128)(2,1)S(1)} %get-tuple-element.18) | data formatting | bytes 524288
  68.3 0.7 %copy.11 = bf16[16,64,128]{2,1,0:T(8,128)(2,1)} copy(bf16[16,64,128]{2,1,0:T(8,128)(2,1)S(1)} %get-tuple-element.19) | data formatting | bytes 524288
Async XLA Ops:
  0.6 1.0 %copy-start = (bf16[64,3,3,256]{3,0,2,1:T(8,128)(2,1)S(1)}, bf16[64,3,3,256]{3,0,2,1:T(8,128)(2,1)}, u32[]{:S(2)}) copy-start(bf16[64,3,3,256]{3,0,2,1:T(8,128)(2,1)} %param.5) | copy-start | bytes 884740
  1.6 1.0 %copy-start.1 = (bf16[64,3,3,256]{3,0,2,1:T(8,128)(2,1)S(1)}, bf16[64,3,3,256]{3,0,2,1:T(8,128)(2,1)}, u32[]{:S(2)}) copy-start(bf16[64,3,3,256]{3,0,2,1:T(8,128)(2,1)} %param.6) | copy-start | bytes 884740
  2.6 0.9 %copy-start.2 = (bf16[16,64,128]{2,1,0:T(8,128)(2,1)S(1)}, bf16[16,64,128]{2,1,0:T(8,128)(2,1)}, u32[]{:S(2)}) copy-start(bf16[16,64,128]{2,1,0:T(8,128)(2,1)} %x_ref.1) | copy-start | bytes 786436
  3.5 0.9 %copy-start.3 = (bf16[16,64,128]{2,1,0:T(8,128)(2,1)S(1)}, bf16[16,64,128]{2,1,0:T(8,128)(2,1)}, u32[]{:S(2)}) copy-start(bf16[16,64,128]{2,1,0:T(8,128)(2,1)} %cot_ref.1) | copy-start | bytes 786436
